TPU v7x, 32 devices: a whole 2x2x4 slice. The times are simulated.
32 devices in a mesh: tok: 8 (over z, y), feat: 4 (over x, core).
Axes of the slice: x: 2, y: 2, z: 4, core: 2. Of those that a mesh axis runs over, the one named last changes fastest.
Arguments:
- tokens: bfloat16 [128, 12288], P('tok', 'feat'), may hold values from -6 to 6
- up_weight: bfloat16 [4, 12288, 3, 3072], P('feat', 'tok'), may hold values from -0.0625 to 0.0625
- down_weight: bfloat16 [4, 12288, 3, 3072], P('feat', 'tok'), may hold values from -0.03125 to 0.03125
- up_left: bfloat16 [12288, 512], P('feat'), may hold values from -0.0546875 to 0.0546875
- up_right: bfloat16 [4, 12288, 512], P('feat', 'tok'), may hold values from -0.25 to 0.25
- down_left: bfloat16 [4, 12288, 512], P('feat', 'tok'), may hold values from -0.02734375 to 0.02734375
- down_right: bfloat16 [512, 12288], P(None, 'feat'), may hold values from -0.25 to 0.25
Outputs:
- mixed: bfloat16 [128, 12288], P('tok', 'feat')
All inputs are finite; a program needn't handle non-finite values.
Results may differ from a plain program's by a relative error of at most 0.0058.
Values may be sent and summed in bfloat16 or wider, within the bound.
A program may use at most 128 MiB of HBM per device.

v0:
```python
import jax
import jax.numpy as jnp
from jax import lax
from jax.sharding import PartitionSpec as P


def from_partner(array, axis, bit):
    return lax.ppermute(array, axis, [(i, i ^ 1 << bit) for i in range(lax.axis_size(axis))])


def per_device(tokens, up_weight, down_weight, up_left, up_right, down_left, down_right):
    levels = lax.axis_size("feat").bit_length() - 1
    gathered = lax.all_gather(tokens, "tok", axis=0, tiled=True)
    pieces = [gathered]
    for level in range(levels):
        pieces.append(from_partner(gathered, "feat", level))
    stacked = jnp.stack(pieces, axis=1)
    code_part = jnp.dot(tokens, up_left, preferred_element_type=jnp.float32)
    code = lax.psum(code_part, "feat").astype(jnp.bfloat16)
    code = lax.all_gather(code, "tok", axis=0, tiled=True)
    pre = jnp.einsum("rkd,tkd->rt", up_weight[0], stacked, preferred_element_type=jnp.float32)
    pre = pre + lax.dot_general(
        up_right[0], code, (((1,), (1,)), ((), ())), preferred_element_type=jnp.float32
    )
    hidden = jax.nn.gelu(pre, approximate=False).astype(jnp.bfloat16)
    local_down = down_weight[0]
    terms = jnp.einsum("rt,rkd->tkd", hidden, local_down, preferred_element_type=jnp.float32)
    total = terms[:, 0, :]
    for level in range(levels):
        total = total + from_partner(terms[:, level + 1, :], "feat", level)
    back_part = lax.dot_general(
        hidden, down_left[0], (((0,), (0,)), ((), ())), preferred_element_type=jnp.float32
    )
    total, back = (
        lax.psum_scatter(total, "tok", scatter_dimension=0, tiled=True),
        lax.psum_scatter(back_part, "tok", scatter_dimension=0, tiled=True),
    )
    back = lax.psum(back, "feat")
    mixed = total + jnp.dot(
        back.astype(jnp.bfloat16), down_right, preferred_element_type=jnp.float32
    )
    return mixed.astype(jnp.bfloat16)


def solution(mesh):
    return jax.shard_map(
        per_device,
        mesh=mesh,
        in_specs=(
            P("tok", "feat"),
            P("feat", "tok", None, None),
            P("feat", "tok", None, None),
            P("feat", None),
            P("feat", "tok", None),
            P("feat", "tok", None),
            P(None, "feat"),
        ),
        out_specs=P("tok", "feat"),
        check_vma=False,
    )
```

profile of v0, /device:TPU:0, one launch (start us, length us, event | category | flops | bytes accessed | tf_op | source)
XLA Modules:
  0.0 267.9 jit_solution(8807828136269477149)
XLA Ops:
  6.5 0.0 copy-start
  6.5 0.0 reduce-scatter.5.cloned.1.call-start
  6.5 36.3 %all_gather.6 = bf16[128,3072]{1,0:T(8,128)(2,1)} all-gather(bf16[16,3072]{1,0:T(8,128)(2,1)} %param.7), channel_id=1, replica_groups=mesh['tok'=8,'feat'=4] {'tok'}, dimensions={0}, use_global_device_ids=true | all-gather | bytes 884736 | tf_op jit(solution)/shard_map/all_gather | solution.py:13
  42.9 1.5 collective-permute-start.1
  44.4 0.0 collective-permute-start
  44.4 2.5 fusion.47
  46.8 17.2 %psum.14 = bf16[16,512]{1,0:T(8,128)(2,1)S(1)} all-reduce(f32[16,512]{1,0:T(8,128)S(1)} %fusion.47), channel_id=1, replica_groups=mesh['tok'=8,'feat'=4] {'feat'}, use_global_device_ids=true, to_apply=%region_0.0 | all-reduce | flops 8192 | bytes 49152 | tf_op jit(solution)/shard_map/psum | solution.py:19
  64.1 30.6 %all_gather.7 = bf16[128,512]{1,0:T(8,128)(2,1)S(1)} all-gather(bf16[16,512]{1,0:T(8,128)(2,1)S(1)} %psum.14), channel_id=1, replica_groups=mesh['tok'=8,'feat'=4] {'tok'}, dimensions={0}, use_global_device_ids=true | all-gather | bytes 147456 | tf_op jit(solution)/shard_map/all_gather | solution.py:20
  94.7 2.9 %fusion.19 = f32[128,1536]{1,0:T(8,128)} fusion(bf16[128,512]{1,0:T(8,128)(2,1)S(1)} %all_gather.7, bf16[1,1536,512]{2,1,0:T(8,128)(2,1)} %param.11), kind=kOutput, calls=%fused_computation.18 | convolution fusion | flops 201326592 | bytes 2490368 | tf_op jit(solution)/shard_map/dot_general | solution.py:22
  97.6 0.0 collective-permute-done.1
  97.6 0.0 collective-permute-done
  97.6 16.9 %fusion.23 = bf16[1536,128]{0,1:T(8,128)(2,1)S(1)} fusion(f32[128,1536]{1,0:T(8,128)} %fusion.19, bf16[1,1536,3,3072]{3,1,2,0:T(8,128)(2,1)} %param.8, bf16[128,1,3072]{2,0,1:T(8,128)(2,1)} %bitcast.2, bf16[128,1,3072]{2,0,1:T(8,128)(2,1)} %bitcast.1, bf16[128,1,3072]{2,0,1:T(8,128)(2,1)} %bitcast), kind=kOutput, calls=%fused_computation.23 | convolution fusion | flops 3639214080 | bytes 31850496 | tf_op jit(solution)/shard_map/rkd,tkd->rt/dot_general | solution.py:21
  114.5 11.1 %fusion = f32[128,3,3072]{2,0,1:T(8,128)S(1)} fusion(bf16[1,1536,3,3072]{3,1,2,0:T(8,128)(2,1)} %param.9, bf16[1536,128]{0,1:T(8,128)(2,1)S(1)} %fusion.23), kind=kOutput, calls=%fused_computation | convolution fusion | flops 3623878656 | bytes 33423360 | tf_op jit(solution)/shard_map/rt,rkd->tkd/dot_general | solution.py:27
  125.6 0.0 copy-start.1
  125.6 0.0 copy-start.2
  125.6 2.0 slice_bitcast_fusion.1
  127.6 1.1 copy-done.1
  128.7 0.0 collective-permute-start.2
  128.7 0.4 collective-permute-start.3
  129.1 0.0 copy-done.2
  129.1 1.1 fusion.17
  130.2 0.0 reduce-scatter.5.cloned.1.call-update
  130.2 0.0 reduce-scatter.3.cloned.1.call-start
  130.3 2.1 collective-permute-done.2
  132.4 33.4 %collective-permute-done.3 = f32[128,3072]{1,0:T(8,128)} collective-permute-done((f32[128,3072]{1,0:T(8,128)}, f32[128,3072]{1,0:T(8,128)}, u32[]{:S(2)}, u32[]{:S(2)}) %collective-permute-start.3) | collective-permute-done | bytes 1572896 | tf_op jit(solution)/shard_map/ppermute | solution.py:8
  165.8 3.9 %fusion.16 = f32[128,3072]{1,0:T(8,128)} fusion(f32[128,3072]{1,0:T(8,128)} %collective-permute-done.3, f32[128,3072]{1,0:T(8,128)} %collective-permute-done.2, f32[128,3,3072]{2,0,1:T(8,128)} %copy-done.1), kind=kLoop, calls=%fused_computation.15 | loop fusion | flops 786432 | bytes 6291456 | tf_op jit(solution)/shard_map/add | solution.py:30
  169.7 0.0 reduce-scatter.3.cloned.1.call-update
  169.7 22.4 %reduce-scatter.5.cloned.1.call-done = f32[16,512]{1,0:T(8,128)} async-done(((f32[128,512]{1,0:T(8,128)}), f32[16,512]{1,0:T(8,128)}) %reduce-scatter.5.cloned.1.call-update) | async-done | bytes 32784 | tf_op jit(solution)/shard_map/reduce_scatter | solution.py:36
  192.1 10.8 %psum.15 = bf16[16,512]{1,0:T(8,128)(2,1)S(1)} all-reduce(f32[16,512]{1,0:T(8,128)} %reduce-scatter.5.cloned.1.call-done), channel_id=1, replica_groups=mesh['tok'=8,'feat'=4] {'feat'}, use_global_device_ids=true, to_apply=%region_3.0 | all-reduce | flops 8192 | bytes 49152 | tf_op jit(solution)/shard_map/psum | solution.py:38
  202.9 0.0 copy-done
  202.9 0.5 fusion.48
  203.4 56.0 %reduce-scatter.3.cloned.1.call-done = f32[16,3072]{1,0:T(8,128)} async-done(((f32[128,3072]{1,0:T(8,128)}), f32[16,3072]{1,0:T(8,128)}) %reduce-scatter.3.cloned.1.call-update) | async-done | bytes 196624 | tf_op jit(solution)/shard_map/reduce_scatter | solution.py:35
  259.4 1.6 add_convert_fusion
Async XLA Ops:
  6.5 196.4 %copy-start = (bf16[512,3072]{1,0:T(8,128)(2,1)S(1)}, bf16[512,3072]{1,0:T(8,128)(2,1)}, u32[]{:S(2)}) copy-start(bf16[512,3072]{1,0:T(8,128)(2,1)} %param.13) | copy-start | bytes 9437188
  6.5 185.6 %reduce-scatter.5.cloned.1.call-start = ((), (), s32[]{:S(2)}) async-start(), calls=%async_computation.3 | async-start | bytes 294912 | tf_op jit(solution)/shard_map/reduce_scatter | solution.py:36
  42.9 54.7 %collective-permute-start.1 = (bf16[128,3072]{1,0:T(8,128)(2,1)}, bf16[128,3072]{1,0:T(8,128)(2,1)}, u32[]{:S(2)}, u32[]{:S(2)}) collective-permute-start(bf16[128,3072]{1,0:T(8,128)(2,1)} %all_gather.6), channel_id=1, source_target_pairs={{0,2},{1,3},{2,0},{3,1},{4,6},{5,7},{6,4},{7,5},{8,10},{9,11},{10,... | collective-permute-start | bytes 2359304 | tf_op jit(solution)/shard_map/ppermute | solution.py:8
  44.4 53.2 %collective-permute-start = (bf16[128,3072]{1,0:T(8,128)(2,1)}, bf16[128,3072]{1,0:T(8,128)(2,1)}, u32[]{:S(2)}, u32[]{:S(2)}) collective-permute-start(bf16[128,3072]{1,0:T(8,128)(2,1)} %all_gather.6), channel_id=1, source_target_pairs={{0,1},{1,0},{2,3},{3,2},{4,5},{5,4},{6,7},{7,6},{8,9},{9,8},{10,11... | collective-permute-start | bytes 2359304 | tf_op jit(solution)/shard_map/ppermute | solution.py:8
  125.6 3.1 %copy-start.1 = (f32[128,3,3072]{2,0,1:T(8,128)}, f32[128,3,3072]{2,0,1:T(8,128)S(1)}, u32[]{:S(2)}) copy-start(f32[128,3,3072]{2,0,1:T(8,128)S(1)} %fusion) | copy-start | bytes 14155780
  125.6 3.5 %copy-start.2 = (bf16[1,1536,512]{2,1,0:T(8,128)(2,1)S(1)}, bf16[1,1536,512]{2,1,0:T(8,128)(2,1)}, u32[]{:S(2)}) copy-start(bf16[1,1536,512]{2,1,0:T(8,128)(2,1)} %param.12) | copy-start | bytes 4718596
  128.7 3.8 %collective-permute-start.2 = (f32[128,3072]{1,0:T(8,128)}, f32[128,3072]{1,0:T(8,128)}, u32[]{:S(2)}, u32[]{:S(2)}) collective-permute-start(f32[128,3072]{1,0:T(8,128)} %get-tuple-element.5), channel_id=1, source_target_pairs={{0,1},{1,0},{2,3},{3,2},{4,5},{5,4},{6,7},{7,6},{8,9},{9,8},{10,11... | collective-permute-start | bytes 4718600 | tf_op jit(solution)/shard_map/ppermute | solution.py:8
  128.7 37.1 %collective-permute-start.3 = (f32[128,3072]{1,0:T(8,128)}, f32[128,3072]{1,0:T(8,128)}, u32[]{:S(2)}, u32[]{:S(2)}) collective-permute-start(f32[128,3072]{1,0:T(8,128)} %get-tuple-element.6), channel_id=1, source_target_pairs={{0,2},{1,3},{2,0},{3,1},{4,6},{5,7},{6,4},{7,5},{8,10},{9,11},{10,... | collective-permute-start | bytes 4718600 | tf_op jit(solution)/shard_map/ppermute | solution.py:8
  130.2 129.2 %reduce-scatter.3.cloned.1.call-start = ((), (), s32[]{:S(2)}) async-start(), calls=%async_computation.2 | async-start | bytes 1769472 | tf_op jit(solution)/shard_map/reduce_scatter | solution.py:35
Sparse Core Ops, SparseCore 0:
  130.4 61.6 reduce-scatter.4
  195.5 63.8 reduce-scatter.2
where the time goes:
time: 268 us
  waiting for transfers between devices  114 us (43%)
  blocking collectives  95 us (35%)
  matrix products  35 us (13%)
  between operations  13.4 us (5%)
  other arithmetic  5.47 us (2%)
  local copies, waits for them, and re-layouts  3.08 us (1%)
    reduce_scatter x1, waiting for transfers between devices, per_device(): lax.psum_scatter(total, 'tok', scatter_dimension=0, tiled=True)  56 us
    all_gather x1, blocking collectives, per_device(): gathered = lax.all_gather(tokens, 'tok', axis=0, tiled=True)  36.3 us
    ppermute x4, waiting for transfers between devices, from_partner(): lax.ppermute(array, axis, [(i, i ^ 1 << bit) for i in range(lax.axis_size...  35.5 us
    all_gather x1, blocking collectives, per_device(): code = lax.all_gather(code, 'tok', axis=0, tiled=True)  30.6 us
    reduce_scatter x1, waiting for transfers between devices, per_device(): lax.psum_scatter(back_part, 'tok', scatter_dimension=0, tiled=True)  22.4 us
    psum x1, blocking collectives, per_device(): code = lax.psum(code_part, 'feat').astype(jnp.bfloat16)  17.2 us
    dot_general x1, matrix products, per_device(): jnp.einsum('rkd,tkd->rt', up_weight[0], stacked, preferred_element_type=j...  16.9 us
    dot_general x1, matrix products, per_device(): jnp.einsum('rt,rkd->tkd', hidden, local_down, preferred_element_type=jnp....  11.1 us
  transfers between devices with their start and end apart: 6, of which 4 were waited for; matrix products, arithmetic and copies ran while one was open for 4% of the time, Pallas kernels for 0%

commit v1 on v0

--- a/solution.py
+++ b/solution.py
@@ -1,14 +1,305 @@
 import jax
 import jax.numpy as jnp
 from jax import lax
+from jax.experimental import pallas as pl
+from jax.experimental.pallas import tpu as pltpu
 from jax.sharding import PartitionSpec as P
+
+F32, BF16 = jnp.float32, jnp.bfloat16
+MESH = pl.DeviceIdType.MESH
+PLANES = 4
+N_COPIES = 128
+
+
+def nt_dot(a, b):
+    return lax.dot_general(a, b, (((1,), (1,)), ((), ())), preferred_element_type=F32)
+
+
+def gelu(x):
+    return 0.5 * x * (1.0 + lax.erf(x * 0.7071067811865476))
+
+
+def fused_kernel(
+    tokens, up, down, up_left, up_right, down_left, down_right, out,
+    blocks, weights, ul, ur, dl, dr, pre, hidden,
+    code_in, code_own, code_all, back_out, back_in, feat_in, base,
+    p2, p1, p1_in, q0, yout, xdiag, ydiag, xfull, yfull, zout, zin,
+    send_sem, recv_sem, local_sem,
+):
+    rows = tokens.shape[0]
+    db, units = up.shape[2], up.shape[1]
+    half = db // 2
+    tok, feat = lax.axis_index("tok"), lax.axis_index("feat")
+    z, y = lax.div(tok, 2), lax.rem(tok, 2)
+    oy = 1 - y
+
+    def fetch(n, src, dst):
+        copy = pltpu.make_async_copy(src, dst, local_sem.at[n])
+        copy.start()
+        return copy
+
+    got_tokens = fetch(0, tokens, blocks.at[0, tok])
+    got_ul = fetch(1, up_left, ul)
+    got_up = [fetch(2 + k, up.at[k], weights.at[k]) for k in range(3)]
+    got_ur = fetch(5, up_right, ur)
+    got_dl = fetch(6, down_left, dl)
+    got_down = {2: fetch(7, down.at[2], weights.at[3])}
+    got_dr = fetch(8, down_right, dr)
+
+    def tok_peer(e):
+        return {"tok": lax.bitwise_xor(tok, e), "feat": feat}
+
+    def feat_peer(e):
+        return {"tok": tok, "feat": lax.bitwise_xor(feat, e)}
+
+    to_y, to_x, to_sib = tok_peer(1), feat_peer(2), feat_peer(1)
+    barrier = pltpu.get_barrier_semaphore()
+    peers = [tok_peer(e) for e in range(1, 2 * PLANES)] + [feat_peer(e) for e in range(1, 4)]
+    for peer in peers:
+        pl.semaphore_signal(barrier, inc=1, device_id=peer, device_id_type=MESH)
+    pl.semaphore_wait(barrier, len(peers))
+
+    sent = []
+
+    def send(src, dst, peer):
+        n = len(sent)
+        copy = pltpu.make_async_remote_copy(
+            src_ref=src, dst_ref=dst, send_sem=send_sem.at[n], recv_sem=recv_sem.at[n],
+            device_id=peer, device_id_type=MESH)
+        copy.start()
+        sent.append(copy)
+        return copy
+
+    h0, h1 = pl.ds(0, half), pl.ds(half, half)
+    ys, xs, zs, sibs, diag = {}, {}, {}, [], []
+
+    def spread(src, t, d):
+        ys[d] = send(src, blocks.at[0, t], to_y)
+        xs[d] = send(src, blocks.at[2, t], to_x)
+        sibs.append(send(src, blocks.at[1, t], to_sib))
+
+    def at(d, row):
+        return 2 * lax.bitwise_xor(z, d) + row
+
+    spread(tokens, tok, 0)
+    for d in range(1, PLANES):
+        zs[d] = send(tokens, blocks.at[0, tok], tok_peer(2 * d))
+    got_tokens.wait()
+    got_ul.wait()
+    code_in[feat] = jnp.dot(blocks[0, tok], ul[...], preferred_element_type=F32)
+    code_parts = [send(code_in.at[feat], code_in.at[feat], feat_peer(e)) for e in range(1, 4)]
+
+    def from_z(d):
+        zs[d].wait_recv()
+        t = at(d, y)
+        spread(blocks.at[0, t], t, d)
+
+    def from_yx(d):
+        ys[d].wait_recv()
+        t = at(d, oy)
+        sibs.append(send(blocks.at[0, t], blocks.at[1, t], to_sib))
+        diag.append(send(blocks.at[0, t, :, h0], blocks.at[2, t, :, h0], to_x))
+        xs[d].wait_recv()
+        t = at(d, y)
+        diag.append(send(blocks.at[2, t, :, h1], blocks.at[2, t, :, h1], to_y))
+
+    from_z(1)
+    from_yx(0)
+    from_z(2)
+    for copy in code_parts:
+        copy.wait_recv()
+    code_all[tok] = (code_in[0] + code_in[1] + code_in[2] + code_in[3]).astype(BF16)
+    codes = [send(code_all.at[tok], code_all.at[tok], tok_peer(e)) for e in range(1, 2 * PLANES)]
+    from_yx(1)
+    from_z(3)
+    from_yx(2)
+    from_yx(3)
+
+    step = 256
+    count = 2 * PLANES * rows
+
+    def up_part(k, finish):
+        got_up[k].wait()
+
+        def body(j, carry):
+            part = pl.ds(pl.multiple_of(j * step, step), step)
+            value = nt_dot(blocks[k].reshape(count, db), weights[k, part, :])
+            finish(part, value)
+            return carry
+
+        lax.fori_loop(0, units // step, body, 0)
+
+    def first(part, value):
+        pre[:, part] = value
+
+    def more(part, value):
+        pre[:, part] += value
+
+    def last(part, value):
+        low_rank = nt_dot(code_all[...].reshape(count, -1), ur[part, :])
+        hidden[:, part] = gelu(pre[:, part] + value + low_rank).astype(BF16)
+
+    up_part(0, first)
+    got_down[1] = fetch(9, down.at[1], weights.at[0])
+    for copy in sibs:
+        copy.wait_recv()
+    up_part(1, more)
+    got_down[0] = fetch(10, down.at[0], weights.at[1])
+    for copy in diag + codes:
+        copy.wait_recv()
+    got_ur.wait()
+    up_part(2, last)
+
+    got_dl.wait()
+    back_out[...] = jnp.dot(
+        hidden[...], dl[...], preferred_element_type=F32).astype(BF16).reshape(back_out.shape)
+    backs = []
+    for e in range(1, 2 * PLANES):
+        other = lax.bitwise_xor(tok, e)
+        backs.append(send(back_out.at[other], back_in.at[e], tok_peer(e)))
+
+    width = 512
+    n_half = half // width
+    order = [c + s * n_half for c in range(n_half) for s in range(2)]
+    slots = {2: 3, 1: 0, 0: 1}
+
+    def cols_of(c):
+        return pl.ds(c * width, width)
+
+    def down_part(k, c):
+        value = jnp.dot(hidden[...], weights[slots[k], :, cols_of(c)], preferred_element_type=F32)
+        return value.reshape(PLANES, 2, rows, width)
+
+    xd, yd, xf, yf, sib = {}, {}, {}, {}, {}
+    got_down[2].wait()
+    for c in order:
+        cols = cols_of(c)
+        p2[:, :, :, cols] = down_part(2, c).astype(BF16)
+        if c < n_half:
+            xd[c] = send(p2.at[:, oy, :, cols], xdiag.at[:, :, cols], to_x)
+            xf[c] = send(p2.at[:, y, :, cols], xfull.at[:, :, cols], to_x)
+        else:
+            there = pl.ds(c * width - half, width)
+            yd[c] = send(p2.at[:, oy, :, cols], ydiag.at[:, :, there], to_y)
+    got_down[1].wait()
+    for c in order:
+        cols = cols_of(c)
+        p1[:, :, :, cols] = down_part(1, c).astype(BF16)
+        sib[c] = send(p1.at[:, :, :, cols], p1_in.at[:, :, :, cols], to_sib)
+        if c >= n_half:
+            here = pl.ds(c * width - half, width)
+            yd[c].wait_recv()
+            total = p2[:, y, :, cols].astype(F32) + ydiag[:, :, here].astype(F32)
+            p2[:, y, :, cols] = total.astype(BF16)
+            xf[c] = send(p2.at[:, y, :, cols], xfull.at[:, :, cols], to_x)
+    got_down[0].wait()
+    for c in order:
+        cols = cols_of(c)
+        value = down_part(0, c)
+        sib[c].wait_recv()
+        q0[:, :, :, cols] = value + p1_in[:, :, :, cols].astype(F32)
+        away = q0[:, oy, :, cols]
+        if c < n_half:
+            xd[c].wait_recv()
+            away = away + xdiag[:, :, cols].astype(F32)
+        yout[:, :, cols] = away.astype(BF16)
+        yf[c] = send(yout.at[:, :, cols], yfull.at[:, :, cols], to_y)
+
+    for copy in backs:
+        copy.wait_recv()
+    total = back_out[tok].astype(F32)
+    for e in range(1, 2 * PLANES):
+        total = total + back_in[e].astype(F32)
+    feat_in[feat] = total
+    back_parts = [send(feat_in.at[feat], feat_in.at[feat], feat_peer(e)) for e in range(1, 4)]
+
+    zf = {}
+    for c in order:
+        cols = cols_of(c)
+        xf[c].wait_recv()
+        yf[c].wait_recv()
+        total = q0[:, y, :, cols] + xfull[:, :, cols].astype(F32) + yfull[:, :, cols].astype(F32)
+        q0[:, y, :, cols] = total
+        zout[:, :, cols] = total.astype(BF16)
+        for d in range(1, PLANES):
+            zf[c, d] = send(
+                zout.at[lax.bitwise_xor(z, d), :, cols], zin.at[d, :, cols], tok_peer(2 * d))
+
+    for copy in back_parts:
+        copy.wait_recv()
+    back = (feat_in[0] + feat_in[1] + feat_in[2] + feat_in[3]).astype(BF16)
+    got_dr.wait()
+    base[...] = jnp.dot(back, dr[...], preferred_element_type=F32)
+    for c in order:
+        cols = cols_of(c)
+        total = q0[z, y, :, cols] + base[:, cols]
+        for d in range(1, PLANES):
+            zf[c, d].wait_recv()
+            total = total + zin[d, :, cols].astype(F32)
+        out[:, cols] = total.astype(BF16)
+    for copy in sent:
+        copy.wait_send()
+
+
+def fused(tokens, up_weight, down_weight, up_left, up_right, down_left, down_right):
+    rows, db = tokens.shape
+    units = up_weight.shape[1]
+    rank = up_left.shape[1]
+    n = 2 * PLANES
+    anywhere = pl.BlockSpec(memory_space=pl.ANY)
+    vm = pltpu.VMEM
+    return pl.pallas_call(
+        fused_kernel,
+        out_shape=jax.ShapeDtypeStruct((rows, db), BF16),
+        in_specs=[anywhere] * 7,
+        out_specs=pl.BlockSpec(memory_space=pltpu.VMEM),
+        scratch_shapes=[
+            vm((3, n, rows, db), BF16),
+            vm((4, units, db), BF16),
+            vm((db, rank), BF16),
+            vm((units, rank), BF16),
+            vm((units, rank), BF16),
+            vm((rank, db), BF16),
+            vm((n * rows, units), F32),
+            vm((n * rows, units), BF16),
+            vm((4, rows, rank), F32),
+            vm((rows, rank), F32),
+            vm((n, rows, rank), BF16),
+            vm((n, rows, rank), BF16),
+            vm((n, rows, rank), BF16),
+            vm((4, rows, rank), F32),
+            vm((rows, db), F32),
+            vm((PLANES, 2, rows, db), BF16),
+            vm((PLANES, 2, rows, db), BF16),
+            vm((PLANES, 2, rows, db), BF16),
+            vm((PLANES, 2, rows, db), F32),
+            vm((PLANES, rows, db), BF16),
+            vm((PLANES, rows, db // 2), BF16),
+            vm((PLANES, rows, db // 2), BF16),
+            vm((PLANES, rows, db), BF16),
+            vm((PLANES, rows, db), BF16),
+            vm((PLANES, rows, db), BF16),
+            vm((PLANES, rows, db), BF16),
+            pltpu.SemaphoreType.DMA((N_COPIES,)),
+            pltpu.SemaphoreType.DMA((N_COPIES,)),
+            pltpu.SemaphoreType.DMA((11,)),
+        ],
+        compiler_params=pltpu.CompilerParams(
+            collective_id=0, has_side_effects=True, vmem_limit_bytes=63 * 2**20),
+        name="butterfly",
+    )(
+        tokens,
+        jnp.transpose(up_weight[0], (1, 0, 2)),
+        jnp.transpose(down_weight[0], (1, 0, 2)),
+        up_left, up_right[0], down_left[0], down_right,
+    )
 
 
 def from_partner(array, axis, bit):
     return lax.ppermute(array, axis, [(i, i ^ 1 << bit) for i in range(lax.axis_size(axis))])
 
 
-def per_device(tokens, up_weight, down_weight, up_left, up_right, down_left, down_right):
+def general(tokens, up_weight, down_weight, up_left, up_right, down_left, down_right):
     levels = lax.axis_size("feat").bit_length() - 1
     gathered = lax.all_gather(tokens, "tok", axis=0, tiled=True)
     pieces = [gathered]
@@ -40,6 +331,15 @@
         back.astype(jnp.bfloat16), down_right, preferred_element_type=jnp.float32
     )
     return mixed.astype(jnp.bfloat16)
+
+
+def per_device(tokens, up_weight, *rest):
+    rows, db = tokens.shape
+    small = (lax.axis_size("tok"), lax.axis_size("feat")) == (2 * PLANES, 4)
+    fits = rows % 16 == 0 and db % 1024 == 0 and up_weight.shape[1] % 256 == 0
+    fits = fits and up_weight.shape[1] * db * 8 <= 40 * 2**20
+    form = fused if small and fits else general
+    return form(tokens, up_weight, *rest)
 
 
 def solution(mesh):

time: 268 us -> 59.4 us (0.22)
  waiting for transfers between devices: 114 us -> 0 us
  blocking collectives: 95 us -> 0 us
  Pallas kernels: 0 us -> 57.7 us
  matrix products: 35 us -> 0 us
  between operations: 13.4 us -> 0.01 us
  other arithmetic: 5.47 us -> 0 us
    reduce_scatter x2 -> x0, waiting for transfers between devices: 78.4 us -> none  [the longest x1 56 us: per_device(): lax.psum_scatter(total, 'tok', scatter_dimension=0, tiled=True)]
    all_gather x2 -> x0, blocking collectives: 67 us -> none  [the longest x1 36.3 us: per_device(): gathered = lax.all_gather(tokens, 'tok', axis=0, tiled=True)]
    pallas_call x0 -> x1, Pallas kernels: none -> 57.7 us  [fused(): pl.pallas_call(fused_kernel, out_shape=jax.ShapeDtypeStruct((rows, db), B...]
    ppermute x4 -> x0, waiting for transfers between devices: 35.5 us -> none  [from_partner(): lax.ppermute(array, axis, [(i, i ^ 1 << bit) for i in range(lax.axis_size...]
    dot_general x6 -> x0, matrix products: 35 us -> none  [the longest x1 16.9 us: per_device(): jnp.einsum('rkd,tkd->rt', up_weight[0], stacked, preferred_element_type=j...]
    psum x2 -> x0, blocking collectives: 28 us -> none  [the longest x1 17.2 us: per_device(): code = lax.psum(code_part, 'feat').astype(jnp.bfloat16)]
    add x1 -> x0, other arithmetic: 3.88 us -> none  [per_device(): total = total + from_partner(terms[:, level + 1, :], 'feat', level)]
  transfers between devices with their start and end apart: 6 -> 0, of which waited for: 4 -> 0; matrix products, arithmetic and copies ran while one was open for 4% -> 0% of each run, Pallas kernels for 0% -> 0%
where the time goes in v1:
time: 59.4 us; the launch traced here: 59.2 us
  Pallas kernels  57.7 us (97%)
  local copies, waits for them, and re-layouts  1.54 us (3%)
    pallas_call x1, Pallas kernels, fused(): pl.pallas_call(fused_kernel, out_shape=jax.ShapeDtypeStruct((rows, db), B...  57.7 us
    unnamed x1, local copies, waits for them, and re-layouts  1.54 us

profile of v1, /device:TPU:0, one launch (start us, length us, event | category | flops | bytes accessed | tf_op | source)
XLA Modules:
  0.0 59.2 jit_solution(1576352391298594146)
XLA Ops:
  0.0 57.7 %butterfly.1 = bf16[16,3072]{1,0:T(8,128)(2,1)} custom-call(bf16[16,3072]{1,0:T(8,128)(2,1)} %tokens.1, bf16[3,1536,3072]{2,1,0:T(8,128)(2,1)} %bitcast.8, bf16[3,1536,3072]{2,1,0:T(8,128)(2,1)} %bitcast.9, bf16[3072,512]{1,0:T(8,128)(2,1)} %up_left.1, bf16[1536,512]{1,0:T(8,128)(2,1)} %bitcast.10, bf16[1536,512]{1,0:T(8,128)(2,1)} %bitcast.11, ...), custom_call_target="tpu_custom_call" | custom-call | tf_op jit(solution)/shard_map/butterfly/pallas_call | solution.py:251
  57.7 1.5 %copy.9 = bf16[16,3072]{1,0:T(8,128)(2,1)} copy(bf16[16,3072]{1,0:T(8,128)(2,1)} %butterfly.1) | data formatting | bytes 196608

commit v2 on v1

--- a/solution.py
+++ b/solution.py
@@ -22,9 +22,9 @@
 def fused_kernel(
     tokens, up, down, up_left, up_right, down_left, down_right, out,
     blocks, weights, ul, ur, dl, dr, pre, hidden,
-    code_in, code_own, code_all, back_out, back_in, feat_in, base,
+    code_in, code_all, back_out, back_in, feat_in, base,
     p2, p1, p1_in, q0, yout, xdiag, ydiag, xfull, yfull, zout, zin,
-    send_sem, recv_sem, local_sem,
+    send_sem, recv_sem, line_send, line_recv, local_sem,
 ):
     rows = tokens.shape[0]
     db, units = up.shape[2], up.shape[1]
@@ -71,49 +71,69 @@
         return copy
 
     h0, h1 = pl.ds(0, half), pl.ds(half, half)
-    ys, xs, zs, sibs, diag = {}, {}, {}, [], []
-
-    def spread(src, t, d):
-        ys[d] = send(src, blocks.at[0, t], to_y)
-        xs[d] = send(src, blocks.at[2, t], to_x)
+    ys, xs, sibs, diag = [], [], [], []
+    middle = jnp.logical_or(z == 1, z == 2)
+
+    planes = [
+        z,
+        lax.bitwise_xor(z, 1),
+        lax.bitwise_xor(z, jnp.where(middle, 3, 2)),
+        lax.bitwise_xor(z, jnp.where(middle, 2, 3)),
+    ]
+    near, across = tok_peer(2), tok_peer(6)
+
+    def along(n, j, src, dst, peer):
+        return pltpu.make_async_remote_copy(
+            src_ref=src, dst_ref=dst, send_sem=line_send.at[n], recv_sem=line_recv.at[j],
+            device_id=peer, device_id_type=MESH)
+
+    def spread(src, t):
+        ys.append(send(src, blocks.at[0, t], to_y))
+        xs.append(send(src, blocks.at[2, t], to_x))
         sibs.append(send(src, blocks.at[1, t], to_sib))
 
-    def at(d, row):
-        return 2 * lax.bitwise_xor(z, d) + row
-
-    spread(tokens, tok, 0)
-    for d in range(1, PLANES):
-        zs[d] = send(tokens, blocks.at[0, tok], tok_peer(2 * d))
+    own = blocks.at[0, tok]
+    shards = [blocks.at[0, 2 * plane + y] for plane in planes]
+    pair = along(0, 0, tokens, own, near)
+    pair.start()
+    relays = [
+        along(1, 1, tokens, own, across),
+        along(2, 2, shards[1], shards[1], across),
+        along(3, 1, shards[2], shards[2], near),
+        along(4, 2, shards[3], shards[3], near),
+    ]
+
+    def relay(n):
+        pl.when(middle)(lambda: relays[n].start())
+
+    relay(0)
+    spread(tokens, tok)
     got_tokens.wait()
     got_ul.wait()
     code_in[feat] = jnp.dot(blocks[0, tok], ul[...], preferred_element_type=F32)
     code_parts = [send(code_in.at[feat], code_in.at[feat], feat_peer(e)) for e in range(1, 4)]
-
-    def from_z(d):
-        zs[d].wait_recv()
-        t = at(d, y)
-        spread(blocks.at[0, t], t, d)
-
-    def from_yx(d):
-        ys[d].wait_recv()
-        t = at(d, oy)
+    pair.wait_recv()
+    relay(1)
+    spread(shards[1], 2 * planes[1] + y)
+    relays[0].wait_recv()
+    relay(2)
+    spread(shards[2], 2 * planes[2] + y)
+    relays[1].wait_recv()
+    relay(3)
+    spread(shards[3], 2 * planes[3] + y)
+    for j in range(PLANES):
+        ys[j].wait_recv()
+        t = 2 * planes[j] + oy
         sibs.append(send(blocks.at[0, t], blocks.at[1, t], to_sib))
         diag.append(send(blocks.at[0, t, :, h0], blocks.at[2, t, :, h0], to_x))
-        xs[d].wait_recv()
-        t = at(d, y)
+        xs[j].wait_recv()
+        t = 2 * planes[j] + y
         diag.append(send(blocks.at[2, t, :, h1], blocks.at[2, t, :, h1], to_y))
 
-    from_z(1)
-    from_yx(0)
-    from_z(2)
     for copy in code_parts:
         copy.wait_recv()
     code_all[tok] = (code_in[0] + code_in[1] + code_in[2] + code_in[3]).astype(BF16)
     codes = [send(code_all.at[tok], code_all.at[tok], tok_peer(e)) for e in range(1, 2 * PLANES)]
-    from_yx(1)
-    from_z(3)
-    from_yx(2)
-    from_yx(3)
 
     step = 256
     count = 2 * PLANES * rows
@@ -150,6 +170,29 @@
     got_ur.wait()
     up_part(2, last)
 
+    width = 512
+    n_half = half // width
+    order = [c + s * n_half for c in range(n_half) for s in range(2)]
+    slots = {2: 3, 1: 0, 0: 1}
+
+    def cols_of(c):
+        return pl.ds(c * width, width)
+
+    def down_part(k, c):
+        value = jnp.dot(hidden[...], weights[slots[k], :, cols_of(c)], preferred_element_type=F32)
+        return value.reshape(PLANES, 2, rows, width)
+
+    xd, yd, xf, yf, sib = {}, {}, {}, {}, {}
+    got_down[2].wait()
+    for c in order:
+        cols = cols_of(c)
+        p2[:, :, :, cols] = down_part(2, c).astype(BF16)
+        if c < n_half:
+            xd[c] = send(p2.at[:, oy, :, cols], xdiag.at[:, :, cols], to_x)
+            xf[c] = send(p2.at[:, y, :, cols], xfull.at[:, :, cols], to_x)
+        else:
+            there = pl.ds(c * width - half, width)
+            yd[c] = send(p2.at[:, oy, :, cols], ydiag.at[:, :, there], to_y)
     got_dl.wait()
     back_out[...] = jnp.dot(
         hidden[...], dl[...], preferred_element_type=F32).astype(BF16).reshape(back_out.shape)
@@ -158,29 +201,6 @@
         other = lax.bitwise_xor(tok, e)
         backs.append(send(back_out.at[other], back_in.at[e], tok_peer(e)))
 
-    width = 512
-    n_half = half // width
-    order = [c + s * n_half for c in range(n_half) for s in range(2)]
-    slots = {2: 3, 1: 0, 0: 1}
-
-    def cols_of(c):
-        return pl.ds(c * width, width)
-
-    def down_part(k, c):
-        value = jnp.dot(hidden[...], weights[slots[k], :, cols_of(c)], preferred_element_type=F32)
-        return value.reshape(PLANES, 2, rows, width)
-
-    xd, yd, xf, yf, sib = {}, {}, {}, {}, {}
-    got_down[2].wait()
-    for c in order:
-        cols = cols_of(c)
-        p2[:, :, :, cols] = down_part(2, c).astype(BF16)
-        if c < n_half:
-            xd[c] = send(p2.at[:, oy, :, cols], xdiag.at[:, :, cols], to_x)
-            xf[c] = send(p2.at[:, y, :, cols], xfull.at[:, :, cols], to_x)
-        else:
-            there = pl.ds(c * width - half, width)
-            yd[c] = send(p2.at[:, oy, :, cols], ydiag.at[:, :, there], to_y)
     got_down[1].wait()
     for c in order:
         cols = cols_of(c)
@@ -237,6 +257,13 @@
             zf[c, d].wait_recv()
             total = total + zin[d, :, cols].astype(F32)
         out[:, cols] = total.astype(BF16)
+    pair.wait_send()
+
+    @pl.when(middle)
+    def _():
+        for copy in relays:
+            copy.wait_send()
+
     for copy in sent:
         copy.wait_send()
 
@@ -263,7 +290,6 @@
             vm((n * rows, units), F32),
             vm((n * rows, units), BF16),
             vm((4, rows, rank), F32),
-            vm((rows, rank), F32),
             vm((n, rows, rank), BF16),
             vm((n, rows, rank), BF16),
             vm((n, rows, rank), BF16),
@@ -282,6 +308,8 @@
             vm((PLANES, rows, db), BF16),
             pltpu.SemaphoreType.DMA((N_COPIES,)),
             pltpu.SemaphoreType.DMA((N_COPIES,)),
+            pltpu.SemaphoreType.DMA((5,)),
+            pltpu.SemaphoreType.DMA((3,)),
             pltpu.SemaphoreType.DMA((11,)),
         ],
         compiler_params=pltpu.CompilerParams(

time: 59.4 us -> 57.4 us (0.966)
  Pallas kernels: 57.7 us -> 55.8 us
    pallas_call x1, Pallas kernels: 57.7 us -> 55.8 us  [fused(): pl.pallas_call(fused_kernel, out_shape=jax.ShapeDtypeStruct((rows, db), B...]
where the time goes in v2:
time: 57.4 us; the launch traced here: 57.3 us
  Pallas kernels  55.8 us (97%)
  local copies, waits for them, and re-layouts  1.54 us (3%)
    pallas_call x1, Pallas kernels, fused(): pl.pallas_call(fused_kernel, out_shape=jax.ShapeDtypeStruct((rows, db), B...  55.8 us
    unnamed x1, local copies, waits for them, and re-layouts  1.54 us

profile of v2, /device:TPU:0, one launch (start us, length us, event | category | flops | bytes accessed | tf_op | source)
XLA Modules:
  0.0 57.3 jit_solution(10693310881546137579)
XLA Ops:
  0.0 55.8 %butterfly.1 = bf16[16,3072]{1,0:T(8,128)(2,1)} custom-call(bf16[16,3072]{1,0:T(8,128)(2,1)} %tokens.1, bf16[3,1536,3072]{2,1,0:T(8,128)(2,1)} %bitcast.8, bf16[3,1536,3072]{2,1,0:T(8,128)(2,1)} %bitcast.9, bf16[3072,512]{1,0:T(8,128)(2,1)} %up_left.1, bf16[1536,512]{1,0:T(8,128)(2,1)} %bitcast.10, bf16[1536,512]{1,0:T(8,128)(2,1)} %bitcast.11, ...), custom_call_target="tpu_custom_call" | custom-call | tf_op jit(solution)/shard_map/butterfly/pallas_call | solution.py:278
  55.8 1.5 %copy.9 = bf16[16,3072]{1,0:T(8,128)(2,1)} copy(bf16[16,3072]{1,0:T(8,128)(2,1)} %butterfly.1) | data formatting | bytes 196608
